TPU v7x, 32 devices: a whole 2x2x4 slice. The times are simulated.
32 devices in a mesh: wind: 2 (over y), gx: 4 (over z), gy: 2 (over x), gz: 2 (over core).
Axes of the slice: x: 2, y: 2, z: 4, core: 2. Of those that a mesh axis runs over, the one named last changes fastest.
Arguments:
- pressure: bfloat16 [8192, 8192], P(('wind', 'gx'), ('gy', 'gz')), parts along dimension 0, may hold values from -40 to 40
- fir_taps: bfloat16 [257], replicated, may hold values from -0.375 to 0.375
- influence: bfloat16 [256, 4, 4, 512], P(None, ('gy', 'gz'), 'gx'), may hold values from -0.0625 to 0.0625
- mode_impulse: float32 [256, 64], replicated, may hold values from -0.75 to 0.75
- mode_taps: int32 [256], replicated, may hold values from 1 to 64, as said below
Outputs:
- responses: bfloat16 [512, 4096], P(('wind', 'gx', 'gy', 'gz')), parts along dimension 0
- correlation_score: float32 [512, 4, 4, 512], P('wind', ('gy', 'gz'), 'gx'), parts along dimension 0
There are 2 independent parts, one for each index of `wind`. A program takes and returns all parts, laid end to end along the dimension named above; an argument that names none is the same for every part. Nothing has to cross between parts.
Inputs may be any that keep to these rules, and one draw needn't show every extreme that they name: `mode_taps`: some mode keeps all 64 taps.
All inputs are finite; a program needn't handle non-finite values.
Results may differ from a plain program's by a relative error of at most 0.005.
Values may be sent and summed in bfloat16 or wider, within the bound.
A program may use at most 64 MiB of HBM per device.

v0:
```python
import math
import jax
import jax.numpy as jnp
from jax import lax
from jax.sharding import PartitionSpec as P

F32 = jnp.float32
BF16 = jnp.bfloat16


def dot(a, b, contract):
    return lax.dot_general(a, b, (contract, ((), ())), preferred_element_type=F32)


def band_matrix(tap_row, row_count):
    tap_count = tap_row.shape[0]
    extended = jnp.concatenate([tap_row, jnp.zeros((row_count,), tap_row.dtype)])
    flat = jnp.tile(extended, row_count)[: row_count * (row_count + tap_count - 1)]
    return flat.reshape(row_count, row_count + tap_count - 1)


def windows(padded, block, width):
    count = (padded.shape[1] - (width - block)) // block
    return jnp.stack([padded[:, i * block : i * block + width] for i in range(count)], axis=1)


def dynamic_filter(series, impulse, tap_limits):
    impulse_len = impulse.shape[1]
    kept_mask = jnp.arange(impulse_len, dtype=jnp.int32)[None, :] < tap_limits[:, None]
    kernel_taps = jnp.where(kept_mask, impulse, jnp.zeros_like(impulse))[:, ::-1]
    result = lax.conv_general_dilated(
        series[None],
        kernel_taps[:, None, :],
        window_strides=(1,),
        padding=[(impulse_len - 1, 0)],
        dimension_numbers=("NCH", "OIH", "NCH"),
        feature_group_count=series.shape[0],
        precision=lax.Precision.HIGHEST,
    )
    return result[0]


def panel_moments(pressure, halo, band, block):
    rows = pressure.shape[0]
    padded = jnp.concatenate([halo, pressure], axis=0)
    width = band.shape[1]
    parts = [dot(band, padded[o : o + width], ((1,), (0,))) for o in range(0, rows, block)]
    filtered = jnp.concatenate(parts, axis=0).astype(BF16)
    wide = filtered.astype(F32)
    mean = jnp.mean(wide, axis=0)
    spread = jnp.sum(jnp.square(wide - mean[None, :]), axis=0)
    return (mean, spread)


def body(pressure, fir_taps, influence, mode_impulse, mode_taps):
    nx, ng = (lax.axis_size("gx"), lax.axis_size(("gy", "gz")))
    rows, panels = pressure.shape
    total = rows * nx
    rim = fir_taps.shape[0] - 1
    modes = influence.shape[0]
    own = modes // (nx * ng)
    own_panels = panels // nx
    block = min(512, rows)
    lines = lax.all_gather(influence.reshape(modes, -1), "gx", axis=1, tiled=True)
    halo = lax.ppermute(pressure[rows - rim :], "gx", [(i, i + 1) for i in range(nx - 1)])
    raw = dot(lines, pressure, ((1,), (1,)))
    raw = lax.psum_scatter(
        raw.reshape(nx, ng * own, rows), ("gy", "gz"), scatter_dimension=1, tiled=True
    )
    raw = lax.all_to_all(raw, "gx", split_axis=0, concat_axis=0, tiled=True)
    raw = raw.transpose(1, 0, 2).reshape(own, total)
    forward = band_matrix(fir_taps, 512)
    backward = band_matrix(fir_taps[::-1], 512)
    width = forward.shape[1]
    padded = jnp.pad(raw, ((0, 0), (rim, 0)))
    high = padded.astype(BF16)
    low = (padded - high.astype(F32)).astype(BF16)
    loads = sum(
        (
            dot(windows(x, 512, width).reshape(-1, width), backward, ((1,), (1,)))
            for x in (high, low)
        )
    ).reshape(own, total)
    first_mode = lax.axis_index(("gx", "gy", "gz")) * own
    own_impulse = lax.dynamic_slice_in_dim(mode_impulse, first_mode, own, 0)
    own_limits = lax.dynamic_slice_in_dim(mode_taps, first_mode, own, 0)
    responses = dynamic_filter(loads, own_impulse, own_limits).astype(BF16)
    resp_wide = responses.astype(F32)
    mean_mode = jnp.mean(resp_wide, axis=1)
    spread_mode = jnp.sqrt(jnp.mean(jnp.square(resp_wide - mean_mode[:, None]), axis=1) + 1e-06)
    ahead = windows(jnp.pad(responses, ((0, 0), (0, rim))), 512, width).reshape(-1, width)
    back = dot(ahead, forward, ((1,), (1,))).reshape(own, total)
    left = total - 1 - jnp.arange(total, dtype=jnp.int32)
    within = jnp.arange(rim + 1, dtype=jnp.int32)[:, None] <= left[None, :]
    reach = jnp.sum(jnp.where(within, fir_taps.astype(F32)[:, None], 0.0), axis=0)
    scale = 1.0 / (math.sqrt(total) * spread_mode)
    back = ((back - mean_mode[:, None] * reach[None, :]) * scale[:, None]).astype(BF16)
    back = back.reshape(own, nx, rows).transpose(1, 0, 2)
    back = lax.all_to_all(back, "gx", split_axis=0, concat_axis=0, tiled=True)
    back = lax.all_gather(back, ("gy", "gz"), axis=1, tiled=True).reshape(modes, rows)
    cross = dot(back, pressure, ((1,), (0,))).astype(BF16)
    cross = lax.all_to_all(
        cross.reshape(modes, nx, own_panels), "gx", split_axis=1, concat_axis=1, tiled=True
    )
    cross = jnp.sum(cross.astype(F32), axis=1)
    mean_part, square_part = panel_moments(
        pressure, halo, band_matrix(fir_taps[::-1], block), block
    )
    moments = jnp.stack([mean_part, square_part]).reshape(2, nx, own_panels)
    moments = lax.all_to_all(moments, "gx", split_axis=1, concat_axis=1, tiled=True)
    mean_panel = jnp.mean(moments[0], axis=0)
    squares = jnp.sum(moments[1] + rows * jnp.square(moments[0] - mean_panel[None, :]), axis=0)
    spread_panel = jnp.sqrt(squares / total + 1e-06)
    scores = cross / spread_panel[None, :]
    return (responses, scores.reshape(influence.shape))


def solution(mesh):
    return jax.shard_map(
        body,
        mesh=mesh,
        in_specs=(
            P(("wind", "gx"), ("gy", "gz")),
            P(),
            P(None, ("gy", "gz"), "gx", None),
            P(),
            P(),
        ),
        out_specs=(P(("wind", "gx", "gy", "gz"), None), P("wind", ("gy", "gz"), "gx", None)),
        check_vma=False,
    )
```

profile of v0, /device:TPU:0, one launch (start us, length us, event | category | flops | bytes accessed | tf_op | source)
XLA Modules:
  0.0 195.6 jit_solution(10294810391997105271)
XLA Ops:
  8.0 2.3 %slice.128 = bf16[256,2048]{1,0:T(8,128)(2,1)} slice(bf16[1024,2048]{1,0:T(8,128)(2,1)} %param.5), slice={[768:1024], [0:2048]} | slice | bytes 2097152 | tf_op jit(solution)/shard_map/slice | solution.py:65
  10.3 5.9 %collective-permute-start = (bf16[256,2048]{1,0:T(8,128)(2,1)}, bf16[256,2048]{1,0:T(8,128)(2,1)}, u32[]{:S(2)}, u32[]{:S(2)}) collective-permute-start(bf16[256,2048]{1,0:T(8,128)(2,1)} %slice.128), channel_id=1, source_target_pairs={{0,4},{4,8},{8,12},{1,5},{5,9},{9,13},{2,6},{6,10},{10,14},{3,7},{... | collective-permute-start | bytes 3145736 | tf_op jit(solution)/shard_map/ppermute | solution.py:65
  16.9 0.8 reverse
  18.5 1.3 tile.9
  20.9 1.3 tile.11
  22.3 1.6 reshape.135
  23.8 3.7 %fusion.7 = bf16[512,2048]{1,0:T(8,128)(2,1)S(1)} fusion(bf16[512,768]{1,0:T(8,128)(2,1)S(1)} %reshape.132, bf16[1024,2048]{1,0:T(8,128)(2,1)} %param.5), kind=kOutput, calls=%fused_computation.13 | convolution fusion | flops 1611661312 | bytes 6029312 | tf_op jit(solution)/shard_map/dot_general | solution.py:12
  27.5 26.4 %all-gather.3.cloned.1.call-done = bf16[256,1,1,2048]{3,0,2,1:T(8,128)(2,1)} async-done(((bf16[256,1,1,512]{3,0,2,1:T(8,128)(2,1)}), bf16[256,1,1,2048]{3,0,2,1:T(8,128)(2,1)}) %all-gather.3.cloned.1.call-update) | async-done | bytes 1048592 | tf_op jit(solution)/shard_map/all_gather | solution.py:64
  54.0 3.8 %fusion.17 = f32[256,1024]{1,0:T(8,128)S(1)} fusion(bf16[1024,2048]{1,0:T(8,128)(2,1)} %param.5, bf16[256,1,1,2048]{3,0,2,1:T(8,128)(2,1)} %all-gather.3.cloned.1.call-done), kind=kOutput, calls=%fused_computation.26 | convolution fusion | flops 1073741824 | bytes 6291456 | tf_op jit(solution)/shard_map/dot_general | solution.py:12
  57.8 1.7 copy.44
  61.5 5.0 %fusion.6 = bf16[512,2048]{1,0:T(8,128)(2,1)} fusion(bf16[512,768]{1,0:T(8,128)(2,1)S(1)} %reshape.132, bf16[1024,2048]{1,0:T(8,128)(2,1)} %param.5, bf16[256,2048]{1,0:T(8,128)(2,1)} %collective-permute-done), kind=kOutput, calls=%fused_computation.12 | convolution fusion | flops 1617952768 | bytes 8126464 | tf_op jit(solution)/shard_map/dot_general | solution.py:12
  66.5 29.7 %all-reduce.7.cloned.1.call-done = f32[4,64,1024]{2,0,1:T(4,128)} async-done(((f32[4,64,1024]{2,0,1:T(4,128)}), f32[4,64,1024]{2,0,1:T(4,128)}) %all-reduce.7.cloned.1.call-update) | async-done | bytes 1048592
  96.2 1.0 constant_dynamic-slice_fusion
  97.2 0.9 copy.45
  98.0 4.6 %all-to-all-start = ((f32[4,16,1024]{2,1,0:T(8,128)}), f32[4,16,1024]{2,1,0:T(8,128)S(1)}, u32[]{:S(2)}, u32[]{:S(2)}) async-start(f32[4,16,1024]{2,1,0:T(8,128)} %copy.45), calls=%async_computation | async-start | bytes 524288 | tf_op jit(solution)/shard_map/all_to_all | solution.py:70
  102.6 2.2 %convert_reduce_fusion = f32[2048]{0:T(1024)S(1)} fusion(bf16[512,2048]{1,0:T(8,128)(2,1)S(1)} %fusion.7, bf16[512,2048]{1,0:T(8,128)(2,1)} %fusion.6), kind=kLoop, calls=%fused_computation.1 | loop fusion | flops 10483712 | bytes 4202496 | tf_op jit(solution)/shard_map/reduce_sum | solution.py:50
  104.9 6.2 %all-to-all-done = f32[4,16,1024]{2,1,0:T(8,128)S(1)} async-done(((f32[4,16,1024]{2,1,0:T(8,128)}), f32[4,16,1024]{2,1,0:T(8,128)S(1)}, u32[]{:S(2)}, u32[]{:S(2)}) %all-to-all-start) | async-done | bytes 262176 | tf_op jit(solution)/shard_map/all_to_all | solution.py:70
  112.5 2.0 %copy.50 = f32[16,1,8,520]{0,2,3,1:T(8,128)} copy(f32[16,1,8,520]{3,2,0,1:T(8,128)S(1)} %reshape.141) | data formatting | bytes 532480 | tf_op jit(solution)/shard_map/conv_general_dilated | solution.py:31
  114.5 1.0 slice.152
  115.5 12.7 %fusion.11 = bf16[8,520,16]{2,0,1:T(8,128)(2,1)} fusion(f32[16,1,64]{0,1,2:T(1,128)S(1)} %bitcast.169, f32[16,1,7,63]{0,2,3,1:T(8,128)S(1)} %slice.152, f32[16,1,8,520]{0,2,3,1:T(8,128)} %copy.50), kind=kOutput, calls=%fused_computation.17 | convolution fusion | flops 51341952 | bytes 431680 | tf_op jit(solution)/shard_map/conv_general_dilated | solution.py:31
  128.2 1.8 copy.52
  131.4 0.8 fusion.31
  132.2 3.3 %all-to-all-start.1 = ((bf16[4,16,1024]{2,1,0:T(8,128)(2,1)}), bf16[4,16,1024]{2,1,0:T(8,128)(2,1)S(1)}, u32[]{:S(2)}, u32[]{:S(2)}) async-start(bf16[4,16,1024]{2,1,0:T(8,128)(2,1)} %fusion.31), calls=%async_computation.1 | async-start | bytes 262144 | tf_op jit(solution)/shard_map/all_to_all | solution.py:99
  135.5 2.4 %fusion.1 = f32[2048]{0:T(1024)S(1)} fusion(f32[2048]{0:T(1024)S(1)} %broadcast_multiply_fusion, bf16[512,2048]{1,0:T(8,128)(2,1)S(1)} %fusion.7, bf16[512,2048]{1,0:T(8,128)(2,1)} %fusion.6), kind=kLoop, calls=%fused_computation.3 | loop fusion | flops 14678016 | bytes 4210688 | tf_op jit(solution)/shard_map/reduce_sum | solution.py:51
  138.6 2.8 %all-to-all-done.1 = bf16[4,16,1024]{2,1,0:T(8,128)(2,1)S(1)} async-done(((bf16[4,16,1024]{2,1,0:T(8,128)(2,1)}), bf16[4,16,1024]{2,1,0:T(8,128)(2,1)S(1)}, u32[]{:S(2)}, u32[]{:S(2)}) %all-to-all-start.1) | async-done | bytes 131104 | tf_op jit(solution)/shard_map/all_to_all | solution.py:99
  141.4 3.2 %all-to-all-start.3 = ((f32[2,4,512]{2,0,1:T(2,128)}), f32[2,4,512]{2,0,1:T(2,128)S(1)}, u32[]{:S(2)}, u32[]{:S(2)}) async-start(f32[2,4,512]{2,0,1:T(2,128)} %pad_maximum_fusion.5), calls=%async_computation.3 | async-start | bytes 32768 | tf_op jit(solution)/shard_map/all_to_all | solution.py:110
  144.7 7.0 %all_gather.7 = bf16[4,64,1024]{2,1,0:T(8,128)(2,1)S(1)} all-gather(bf16[4,16,1024]{2,1,0:T(8,128)(2,1)S(1)} %all-to-all-done.1), channel_id=1, replica_groups=mesh['wind'=2,'gx'=4,'gy'=2,'gz'=2] {'gy','gz'}, dimensions={1}, use_global_device_ids=true | all-gather | bytes 655360 | tf_op jit(solution)/shard_map/all_gather | solution.py:100
  151.7 3.5 %convolution_convert_fusion = bf16[256,2048]{1,0:T(8,128)(2,1)S(1)} fusion(bf16[256,1024]{1,0:T(8,128)(2,1)S(1)} %bitcast.166, bf16[1024,2048]{1,0:T(8,128)(2,1)} %param.5), kind=kOutput, calls=%fused_computation.14 | convolution fusion | flops 1074266112 | bytes 5767168 | tf_op jit(solution)/shard_map/dot_general | solution.py:12
  155.1 1.1 copy.88
  156.2 5.0 %all-to-all-start.2 = ((bf16[256,4,512]{2,0,1:T(8,128)(2,1)}), bf16[256,4,512]{2,0,1:T(8,128)(2,1)S(1)}, u32[]{:S(2)}, u32[]{:S(2)}) async-start(bf16[256,4,512]{2,0,1:T(8,128)(2,1)} %bitcast.160), calls=%async_computation.2 | async-start | bytes 2097152 | tf_op jit(solution)/shard_map/all_to_all | solution.py:102
  161.3 26.2 %all-to-all-done.2 = bf16[256,4,512]{2,0,1:T(8,128)(2,1)S(1)} async-done(((bf16[256,4,512]{2,0,1:T(8,128)(2,1)}), bf16[256,4,512]{2,0,1:T(8,128)(2,1)S(1)}, u32[]{:S(2)}, u32[]{:S(2)}) %all-to-all-start.2) | async-done | bytes 1048608 | tf_op jit(solution)/shard_map/all_to_all | solution.py:102
  187.6 1.2 reshape_divide_fusion
  (82 shorter events, 8.0 us)
Async XLA Ops:
  7.2 13.4 %copy-start.4 = (s32[256]{0:T(256)S(1)}, s32[256]{0:T(256)}, u32[]{:S(2)}) copy-start(s32[256]{0:T(256)} %param.9) | copy-start | bytes 3076
  7.2 13.5 %copy-start.2 = (f32[256,64]{0,1:T(8,128)S(1)}, f32[256,64]{0,1:T(8,128)}, u32[]{:S(2)}) copy-start(f32[256,64]{0,1:T(8,128)} %param.8) | copy-start | bytes 196612
  7.2 46.8 %all-gather.3.cloned.1.call-start = ((), (), s32[]{:S(2)}) async-start(), calls=%async_computation.4 | async-start | bytes 1310720 | tf_op jit(solution)/shard_map/all_gather | solution.py:64
  7.9 88.3 %all-reduce.7.cloned.1.call-start = ((), (), s32[]{:S(2)}) async-start(), calls=%async_computation.5 | async-start | bytes 2097152
  10.3 51.2 %collective-permute-start = (bf16[256,2048]{1,0:T(8,128)(2,1)}, bf16[256,2048]{1,0:T(8,128)(2,1)}, u32[]{:S(2)}, u32[]{:S(2)}) collective-permute-start(bf16[256,2048]{1,0:T(8,128)(2,1)} %slice.128), channel_id=1, source_target_pairs={{0,4},{4,8},{8,12},{1,5},{5,9},{9,13},{2,6},{6,10},{10,14},{3,7},{... | collective-permute-start | bytes 3145736 | tf_op jit(solution)/shard_map/ppermute | solution.py:65
  27.5 32.7 %copy-start.5 = (u32[32]{0:T(128)S(1)}, u32[32]{0:T(128)}, u32[]{:S(2)}) copy-start(u32[32]{0:T(128)} %constant.69) | copy-start | bytes 388
  98.0 13.0 %all-to-all-start = ((f32[4,16,1024]{2,1,0:T(8,128)}), f32[4,16,1024]{2,1,0:T(8,128)S(1)}, u32[]{:S(2)}, u32[]{:S(2)}) async-start(f32[4,16,1024]{2,1,0:T(8,128)} %copy.45), calls=%async_computation | async-start | bytes 524288 | tf_op jit(solution)/shard_map/all_to_all | solution.py:70
  115.5 14.6 %copy-start.3 = (pred[8,520]{1,0:T(8,128)(4,1)S(1)}, pred[8,520]{1,0:T(8,128)(4,1)}, u32[]{:S(2)}) copy-start(pred[8,520]{1,0:T(8,128)(4,1)} %constant.66) | copy-start | bytes 12484
  115.5 15.3 %copy-start = (bf16[512,768]{1,0:T(8,128)(2,1)S(1)}, bf16[512,768]{1,0:T(8,128)(2,1)}, u32[]{:S(2)}) copy-start(bf16[512,768]{1,0:T(8,128)(2,1)} %reshape.135) | copy-start | bytes 2359300
  130.5 24.6 %copy-start.1 = (bf16[16,4096]{1,0:T(8,128)(2,1)}, bf16[16,4096]{1,0:T(8,128)(2,1)S(1)}, u32[]{:S(2)}) copy-start(bf16[16,4096]{1,0:T(8,128)(2,1)S(1)} %get-tuple-element.3) | copy-start | bytes 393220
  132.2 9.2 %all-to-all-start.1 = ((bf16[4,16,1024]{2,1,0:T(8,128)(2,1)}), bf16[4,16,1024]{2,1,0:T(8,128)(2,1)S(1)}, u32[]{:S(2)}, u32[]{:S(2)}) async-start(bf16[4,16,1024]{2,1,0:T(8,128)(2,1)} %fusion.31), calls=%async_computation.1 | async-start | bytes 262144 | tf_op jit(solution)/shard_map/all_to_all | solution.py:99
  141.4 14.8 %all-to-all-start.3 = ((f32[2,4,512]{2,0,1:T(2,128)}), f32[2,4,512]{2,0,1:T(2,128)S(1)}, u32[]{:S(2)}, u32[]{:S(2)}) async-start(f32[2,4,512]{2,0,1:T(2,128)} %pad_maximum_fusion.5), calls=%async_computation.3 | async-start | bytes 32768 | tf_op jit(solution)/shard_map/all_to_all | solution.py:110
  156.2 31.3 %all-to-all-start.2 = ((bf16[256,4,512]{2,0,1:T(8,128)(2,1)}), bf16[256,4,512]{2,0,1:T(8,128)(2,1)S(1)}, u32[]{:S(2)}, u32[]{:S(2)}) async-start(bf16[256,4,512]{2,0,1:T(8,128)(2,1)} %bitcast.160), calls=%async_computation.2 | async-start | bytes 2097152 | tf_op jit(solution)/shard_map/all_to_all | solution.py:102
Sparse Core Ops, SparseCore 0:
  9.6 44.3 all-gather.2
  59.6 36.5 all-reduce.6
where the time goes:
time: 196 us
  waiting for transfers between devices  92 us (47%)
  matrix products  29.8 us (15%)
  starting transfers between devices  22.2 us (11%)
  local copies, waits for them, and re-layouts  20 us (10%)
  between operations  15.2 us (8%)
  other arithmetic  9.45 us (5%)
  blocking collectives  6.99 us (4%)
    unnamed x3, waiting for transfers between devices  30.4 us
    all_gather x1, waiting for transfers between devices, body(): lax.all_gather(influence.reshape(modes, -1), 'gx', axis=1, tiled=True)  26.4 us
    all_to_all x1, waiting for transfers between devices, body(): lax.all_to_all(cross.reshape(modes, nx, own_panels), 'gx', split_axis=1,...  26.2 us
    dot_general x7, matrix products, dot(): lax.dot_general(a, b, (contract, ((), ())), preferred_element_type=F32)  17.1 us
    conv_general_dilated x1, matrix products, dynamic_filter(): lax.conv_general_dilated(series[None], kernel_taps[:, None, :], window_st...  12.7 us
    all_gather x1, blocking collectives, body(): lax.all_gather(back, ('gy', 'gz'), axis=1, tiled=True).reshape(modes, rows)  6.99 us
    all_to_all x1, waiting for transfers between devices, body(): raw = lax.all_to_all(raw, 'gx', split_axis=0, concat_axis=0, tiled=True)  6.18 us
    ppermute x1, starting transfers between devices, body(): lax.ppermute(pressure[rows - rim:], 'gx', [(i, i + 1) for i in range(nx -...  5.89 us
  transfers between devices with their start and end apart: 7, of which 5 were waited for; matrix products, arithmetic and copies ran while one was open for 18% of the time, Pallas kernels for 0%

commit v1 on v0

--- a/solution.py
+++ b/solution.py
@@ -1,3 +1,4 @@
+import functools
 import math
 import jax
 import jax.numpy as jnp
@@ -6,6 +7,33 @@
 
 F32 = jnp.float32
 BF16 = jnp.bfloat16
+
+
+def place_tracks(array_here, d_out):
+    s_next = list(array_here.shape[1:])
+    s_next[d_out] *= array_here.shape[0]
+    return jnp.moveaxis(array_here, 0, d_out).reshape(s_next)
+
+
+def prepare_array(piece_in, axis_id, along_dim):
+    n_lanes = lax.axis_size(axis_id)
+    store = list(map(lambda m: (m, (m + 1) % n_lanes), range(n_lanes)))
+    seen_now, w1 = ([], [])
+    sheets = [(q, rr) for rr, q in store]
+    for d in range(n_lanes - 1):
+        if d % 2 == 0:
+            seen_now.append(
+                lax.ppermute(seen_now[-1] if seen_now else piece_in, axis_name=axis_id, perm=store)
+            )
+        else:
+            w1.append(lax.ppermute(w1[-1] if w1 else piece_in, axis_name=axis_id, perm=sheets))
+    last = jnp.stack([*seen_now[::-1], piece_in, *w1], 0)
+    q_next = lax.axis_index(axis_id) - len(seen_now)
+    last = last[(jnp.arange(n_lanes) - q_next) % n_lanes]
+    return place_tracks(last, along_dim)
+
+
+match_cards = functools.partial(prepare_array, axis_id=("gy", "gz"), along_dim=1)
 
 
 def dot(a, b, contract):
@@ -97,7 +125,7 @@
     back = ((back - mean_mode[:, None] * reach[None, :]) * scale[:, None]).astype(BF16)
     back = back.reshape(own, nx, rows).transpose(1, 0, 2)
     back = lax.all_to_all(back, "gx", split_axis=0, concat_axis=0, tiled=True)
-    back = lax.all_gather(back, ("gy", "gz"), axis=1, tiled=True).reshape(modes, rows)
+    back = match_cards(back).reshape(modes, rows)
     cross = dot(back, pressure, ((1,), (0,))).astype(BF16)
     cross = lax.all_to_all(
         cross.reshape(modes, nx, own_panels), "gx", split_axis=1, concat_axis=1, tiled=True

time: 196 us -> 198 us (1.010)
  blocking collectives: 6.99 us -> 0 us
  waiting for transfers between devices: 92 us -> 98.6 us
    all_gather x1 -> x0, blocking collectives: 6.99 us -> none  [body(): lax.all_gather(back, ('gy', 'gz'), axis=1, tiled=True).reshape(modes, rows)]
    unnamed x3, waiting for transfers between devices: 30.4 us -> 33.7 us
    all_to_all x1, waiting for transfers between devices: 6.18 us -> 3.44 us  [body(): raw = lax.all_to_all(raw, 'gx', split_axis=0, concat_axis=0, tiled=True)]
    ppermute x0 -> x3, waiting for transfers between devices: none -> 2.65 us  [the longest x2 2.65 us: prepare_array(): lax.ppermute(seen_now[-1] if seen_now else piece_in, axis_name=axis_id, p...]
  transfers between devices with their start and end apart: 7 -> 10, of which waited for: 5 -> 7; matrix products, arithmetic and copies ran while one was open for 18% -> 19% of each run, Pallas kernels for 0% -> 0%
where the time goes in v1:
time: 198 us; the launch traced here: 197 us
  waiting for transfers between devices  98.6 us (50%)
  matrix products  29.7 us (15%)
  starting transfers between devices  23.6 us (12%)
  local copies, waits for them, and re-layouts  20.7 us (10%)
  between operations  15.3 us (8%)
  other arithmetic  9.54 us (5%)
    unnamed x3, waiting for transfers between devices  33.7 us
    all_gather x1, waiting for transfers between devices, body(): lax.all_gather(influence.reshape(modes, -1), 'gx', axis=1, tiled=True)  28 us
    all_to_all x1, waiting for transfers between devices, body(): lax.all_to_all(cross.reshape(modes, nx, own_panels), 'gx', split_axis=1,...  26.8 us
    dot_general x7, matrix products, dot(): lax.dot_general(a, b, (contract, ((), ())), preferred_element_type=F32)  17.1 us
    conv_general_dilated x1, matrix products, dynamic_filter(): lax.conv_general_dilated(series[None], kernel_taps[:, None, :], window_st...  12.7 us
    ppermute x1, starting transfers between devices, body(): lax.ppermute(pressure[rows - rim:], 'gx', [(i, i + 1) for i in range(nx -...  5.91 us
    conv_general_dilated x4, local copies, waits for them, and re-layouts, dynamic_filter(): lax.conv_general_dilated(series[None], kernel_taps[:, None, :], window_st...  5.04 us
    all_to_all x1, starting transfers between devices, body(): lax.all_to_all(cross.reshape(modes, nx, own_panels), 'gx', split_axis=1,...  4.71 us
  transfers between devices with their start and end apart: 10, of which 7 were waited for; matrix products, arithmetic and copies ran while one was open for 19% of the time, Pallas kernels for 0%

profile of v1, /device:TPU:0, one launch (start us, length us, event | category | flops | bytes accessed | tf_op | source)
XLA Modules:
  0.0 197.4 jit_solution(11541565003707102893)
XLA Ops:
  8.0 2.4 %slice.128 = bf16[256,2048]{1,0:T(8,128)(2,1)} slice(bf16[1024,2048]{1,0:T(8,128)(2,1)} %param.5), slice={[768:1024], [0:2048]} | slice | bytes 2097152 | tf_op jit(solution)/shard_map/slice | solution.py:93
  10.3 5.9 %collective-permute-start.3 = (bf16[256,2048]{1,0:T(8,128)(2,1)}, bf16[256,2048]{1,0:T(8,128)(2,1)}, u32[]{:S(2)}, u32[]{:S(2)}) collective-permute-start(bf16[256,2048]{1,0:T(8,128)(2,1)} %slice.128), channel_id=1, source_target_pairs={{0,4},{4,8},{8,12},{1,5},{5,9},{9,13},{2,6},{6,10},{10,14},{3,7},{... | collective-permute-start | bytes 3145736 | tf_op jit(solution)/shard_map/ppermute | solution.py:93
  18.5 1.3 tile.9
  20.9 1.3 tile.11
  22.3 1.6 reshape.181
  26.0 28.0 %all-gather.3.cloned.1.call-done = bf16[256,1,1,2048]{3,0,2,1:T(8,128)(2,1)} async-done(((bf16[256,1,1,512]{3,0,2,1:T(8,128)(2,1)}), bf16[256,1,1,2048]{3,0,2,1:T(8,128)(2,1)}) %all-gather.3.cloned.1.call-update) | async-done | bytes 1048592 | tf_op jit(solution)/shard_map/all_gather | solution.py:92
  54.0 3.8 %fusion.17 = f32[256,1024]{1,0:T(8,128)S(1)} fusion(bf16[1024,2048]{1,0:T(8,128)(2,1)} %param.5, bf16[256,1,1,2048]{3,0,2,1:T(8,128)(2,1)} %all-gather.3.cloned.1.call-done), kind=kOutput, calls=%fused_computation.27 | convolution fusion | flops 1073741824 | bytes 6291456 | tf_op jit(solution)/shard_map/dot_general | solution.py:40
  57.8 1.7 copy.55
  59.5 3.7 %fusion.7 = bf16[512,2048]{1,0:T(8,128)(2,1)S(1)} fusion(bf16[512,768]{1,0:T(8,128)(2,1)S(1)} %reshape.178, bf16[1024,2048]{1,0:T(8,128)(2,1)} %param.5), kind=kOutput, calls=%fused_computation.14 | convolution fusion | flops 1611661312 | bytes 6029312 | tf_op jit(solution)/shard_map/dot_general | solution.py:40
  63.2 33.0 %all-reduce.7.cloned.1.call-done = f32[4,64,1024]{2,0,1:T(4,128)} async-done(((f32[4,64,1024]{2,0,1:T(4,128)}), f32[4,64,1024]{2,0,1:T(4,128)}) %all-reduce.7.cloned.1.call-update) | async-done | bytes 1048592
  96.2 1.0 constant_dynamic-slice_fusion
  97.2 0.9 copy.56
  98.0 4.6 %all-to-all-start = ((f32[4,16,1024]{2,1,0:T(8,128)}), f32[4,16,1024]{2,1,0:T(8,128)S(1)}, u32[]{:S(2)}, u32[]{:S(2)}) async-start(f32[4,16,1024]{2,1,0:T(8,128)} %copy.56), calls=%async_computation | async-start | bytes 524288 | tf_op jit(solution)/shard_map/all_to_all | solution.py:98
  102.6 5.0 %fusion.6 = bf16[512,2048]{1,0:T(8,128)(2,1)} fusion(bf16[512,768]{1,0:T(8,128)(2,1)S(1)} %reshape.178, bf16[1024,2048]{1,0:T(8,128)(2,1)} %param.5, bf16[256,2048]{1,0:T(8,128)(2,1)} %collective-permute-done.3), kind=kOutput, calls=%fused_computation.13 | convolution fusion | flops 1617952768 | bytes 8126464 | tf_op jit(solution)/shard_map/dot_general | solution.py:40
  107.6 3.4 %all-to-all-done = f32[4,16,1024]{2,1,0:T(8,128)S(1)} async-done(((f32[4,16,1024]{2,1,0:T(8,128)}), f32[4,16,1024]{2,1,0:T(8,128)S(1)}, u32[]{:S(2)}, u32[]{:S(2)}) %all-to-all-start) | async-done | bytes 262176 | tf_op jit(solution)/shard_map/all_to_all | solution.py:98
  112.5 2.0 %copy.61 = f32[16,1,8,520]{0,2,3,1:T(8,128)} copy(f32[16,1,8,520]{3,2,0,1:T(8,128)S(1)} %reshape.186) | data formatting | bytes 532480 | tf_op jit(solution)/shard_map/conv_general_dilated | solution.py:59
  114.5 1.0 slice.154
  115.5 12.7 %fusion.11 = bf16[8,520,16]{2,0,1:T(8,128)(2,1)} fusion(f32[16,1,64]{0,1,2:T(1,128)S(1)} %bitcast.181, f32[16,1,7,63]{0,2,3,1:T(8,128)S(1)} %slice.154, f32[16,1,8,520]{0,2,3,1:T(8,128)} %copy.61), kind=kOutput, calls=%fused_computation.18 | convolution fusion | flops 51341952 | bytes 431680 | tf_op jit(solution)/shard_map/conv_general_dilated | solution.py:59
  128.2 1.8 copy.63
  131.3 0.8 fusion.31
  132.2 3.3 %all-to-all-start.1 = ((bf16[4,16,1024]{2,1,0:T(8,128)(2,1)}), bf16[4,16,1024]{2,1,0:T(8,128)(2,1)S(1)}, u32[]{:S(2)}, u32[]{:S(2)}) async-start(bf16[4,16,1024]{2,1,0:T(8,128)(2,1)} %fusion.31), calls=%async_computation.1 | async-start | bytes 262144 | tf_op jit(solution)/shard_map/all_to_all | solution.py:127
  135.5 2.2 %convert_reduce_fusion = f32[2048]{0:T(1024)S(1)} fusion(bf16[512,2048]{1,0:T(8,128)(2,1)S(1)} %fusion.7, bf16[512,2048]{1,0:T(8,128)(2,1)} %fusion.6), kind=kLoop, calls=%fused_computation.2 | loop fusion | flops 10483712 | bytes 4202496 | tf_op jit(solution)/shard_map/reduce_sum | solution.py:78
  137.7 3.7 %all-to-all-done.1 = bf16[4,16,1024]{2,1,0:T(8,128)(2,1)S(1)} async-done(((bf16[4,16,1024]{2,1,0:T(8,128)(2,1)}), bf16[4,16,1024]{2,1,0:T(8,128)(2,1)S(1)}, u32[]{:S(2)}, u32[]{:S(2)}) %all-to-all-start.1) | async-done | bytes 131104 | tf_op jit(solution)/shard_map/all_to_all | solution.py:127
  141.4 1.7 collective-permute-start.2
  143.1 2.6 %collective-permute-done = bf16[4,16,1024]{2,1,0:T(8,128)(2,1)S(1)} collective-permute-done((bf16[4,16,1024]{2,1,0:T(8,128)(2,1)S(1)}, bf16[4,16,1024]{2,1,0:T(8,128)(2,1)S(1)}, u32[]{:S(2)}, u32[]{:S(2)}) %collective-permute-start) | collective-permute-done | bytes 131104 | tf_op jit(solution)/shard_map/ppermute | solution.py:26
  145.8 2.4 %fusion.1 = f32[2048]{0:T(1024)S(1)} fusion(f32[2048]{0:T(1024)S(1)} %broadcast_multiply_fusion, bf16[512,2048]{1,0:T(8,128)(2,1)S(1)} %fusion.7, bf16[512,2048]{1,0:T(8,128)(2,1)} %fusion.6), kind=kLoop, calls=%fused_computation.4 | loop fusion | flops 14678016 | bytes 4210688 | tf_op jit(solution)/shard_map/reduce_sum | solution.py:79
  148.8 3.3 %all-to-all-start.3 = ((f32[2,4,512]{2,0,1:T(2,128)}), f32[2,4,512]{2,0,1:T(2,128)S(1)}, u32[]{:S(2)}, u32[]{:S(2)}) async-start(f32[2,4,512]{2,0,1:T(2,128)} %pad_maximum_fusion.6), calls=%async_computation.3 | async-start | bytes 32768 | tf_op jit(solution)/shard_map/all_to_all | solution.py:138
  152.8 3.5 %convolution_convert_fusion = bf16[256,2048]{1,0:T(8,128)(2,1)S(1)} fusion(bf16[256,1024]{1,0:T(8,128)(2,1)S(1)} %bitcast.174, bf16[1024,2048]{1,0:T(8,128)(2,1)} %param.5), kind=kOutput, calls=%fused_computation.15 | convolution fusion | flops 1074266112 | bytes 5767168 | tf_op jit(solution)/shard_map/dot_general | solution.py:40
  156.3 1.1 copy.100
  157.7 4.7 %all-to-all-start.2 = ((bf16[256,4,512]{2,0,1:T(8,128)(2,1)}), bf16[256,4,512]{2,0,1:T(8,128)(2,1)S(1)}, u32[]{:S(2)}, u32[]{:S(2)}) async-start(bf16[256,4,512]{2,0,1:T(8,128)(2,1)} %bitcast.167), calls=%async_computation.2 | async-start | bytes 2097152 | tf_op jit(solution)/shard_map/all_to_all | solution.py:130
  162.5 26.8 %all-to-all-done.2 = bf16[256,4,512]{2,0,1:T(8,128)(2,1)S(1)} async-done(((bf16[256,4,512]{2,0,1:T(8,128)(2,1)}), bf16[256,4,512]{2,0,1:T(8,128)(2,1)S(1)}, u32[]{:S(2)}, u32[]{:S(2)}) %all-to-all-start.2) | async-done | bytes 1048608 | tf_op jit(solution)/shard_map/all_to_all | solution.py:130
  189.4 1.2 reshape_divide_fusion
  (92 shorter events, 9.9 us)
Async XLA Ops:
  7.2 13.5 %copy-start.4 = (s32[256]{0:T(256)S(1)}, s32[256]{0:T(256)}, u32[]{:S(2)}) copy-start(s32[256]{0:T(256)} %param.9) | copy-start | bytes 3076
  7.2 13.6 %copy-start.2 = (f32[256,64]{0,1:T(8,128)S(1)}, f32[256,64]{0,1:T(8,128)}, u32[]{:S(2)}) copy-start(f32[256,64]{0,1:T(8,128)} %param.8) | copy-start | bytes 196612
  7.2 46.8 %all-gather.3.cloned.1.call-start = ((), (), s32[]{:S(2)}) async-start(), calls=%async_computation.4 | async-start | bytes 1310720 | tf_op jit(solution)/shard_map/all_gather | solution.py:92
  7.9 88.3 %all-reduce.7.cloned.1.call-start = ((), (), s32[]{:S(2)}) async-start(), calls=%async_computation.5 | async-start | bytes 2097152
  10.3 92.3 %collective-permute-start.3 = (bf16[256,2048]{1,0:T(8,128)(2,1)}, bf16[256,2048]{1,0:T(8,128)(2,1)}, u32[]{:S(2)}, u32[]{:S(2)}) collective-permute-start(bf16[256,2048]{1,0:T(8,128)(2,1)} %slice.128), channel_id=1, source_target_pairs={{0,4},{4,8},{8,12},{1,5},{5,9},{9,13},{2,6},{6,10},{10,14},{3,7},{... | collective-permute-start | bytes 3145736 | tf_op jit(solution)/shard_map/ppermute | solution.py:93
  20.0 4.8 %copy-start.5 = (u32[32]{0:T(128)S(1)}, u32[32]{0:T(128)}, u32[]{:S(2)}) copy-start(u32[32]{0:T(128)} %constant.85) | copy-start | bytes 388
  98.0 13.0 %all-to-all-start = ((f32[4,16,1024]{2,1,0:T(8,128)}), f32[4,16,1024]{2,1,0:T(8,128)S(1)}, u32[]{:S(2)}, u32[]{:S(2)}) async-start(f32[4,16,1024]{2,1,0:T(8,128)} %copy.56), calls=%async_computation | async-start | bytes 524288 | tf_op jit(solution)/shard_map/all_to_all | solution.py:98
  115.5 14.5 %copy-start.3 = (pred[8,520]{1,0:T(8,128)(4,1)S(1)}, pred[8,520]{1,0:T(8,128)(4,1)}, u32[]{:S(2)}) copy-start(pred[8,520]{1,0:T(8,128)(4,1)} %constant.82) | copy-start | bytes 12484
  115.5 15.3 %copy-start = (bf16[512,768]{1,0:T(8,128)(2,1)S(1)}, bf16[512,768]{1,0:T(8,128)(2,1)}, u32[]{:S(2)}) copy-start(bf16[512,768]{1,0:T(8,128)(2,1)} %reshape.181) | copy-start | bytes 2359300
  130.4 17.8 %copy-start.1 = (bf16[16,4096]{1,0:T(8,128)(2,1)}, bf16[16,4096]{1,0:T(8,128)(2,1)S(1)}, u32[]{:S(2)}) copy-start(bf16[16,4096]{1,0:T(8,128)(2,1)S(1)} %get-tuple-element.3) | copy-start | bytes 393220
  132.2 9.2 %all-to-all-start.1 = ((bf16[4,16,1024]{2,1,0:T(8,128)(2,1)}), bf16[4,16,1024]{2,1,0:T(8,128)(2,1)S(1)}, u32[]{:S(2)}, u32[]{:S(2)}) async-start(bf16[4,16,1024]{2,1,0:T(8,128)(2,1)} %fusion.31), calls=%async_computation.1 | async-start | bytes 262144 | tf_op jit(solution)/shard_map/all_to_all | solution.py:127
  141.4 4.4 %collective-permute-start = (bf16[4,16,1024]{2,1,0:T(8,128)(2,1)S(1)}, bf16[4,16,1024]{2,1,0:T(8,128)(2,1)S(1)}, u32[]{:S(2)}, u32[]{:S(2)}) collective-permute-start(bf16[4,16,1024]{2,1,0:T(8,128)(2,1)S(1)} %all-to-all-done.1), channel_id=1, source_target_pairs={{0,1},{1,2},{2,3},{3,0},{4,5},{5,6},{6,7},{7,4},{8,9},{9,10},{10,1... | collective-permute-start | bytes 393224 | tf_op jit(solution)/shard_map/ppermute | solution.py:26
  141.4 10.7 %collective-permute-start.2 = (bf16[4,16,1024]{2,1,0:T(8,128)(2,1)S(1)}, bf16[4,16,1024]{2,1,0:T(8,128)(2,1)S(1)}, u32[]{:S(2)}, u32[]{:S(2)}) collective-permute-start(bf16[4,16,1024]{2,1,0:T(8,128)(2,1)S(1)} %all-to-all-done.1), channel_id=1, source_target_pairs={{1,0},{2,1},{3,2},{0,3},{5,4},{6,5},{7,6},{4,7},{9,8},{10,9},{11,1... | collective-permute-start | bytes 393224 | tf_op jit(solution)/shard_map/ppermute | solution.py:29
  145.8 6.3 %collective-permute-start.1 = (bf16[4,16,1024]{2,1,0:T(8,128)(2,1)S(1)}, bf16[4,16,1024]{2,1,0:T(8,128)(2,1)S(1)}, u32[]{:S(2)}, u32[]{:S(2)}) collective-permute-start(bf16[4,16,1024]{2,1,0:T(8,128)(2,1)S(1)} %collective-permute-done), channel_id=1, source_target_pairs={{0,1},{1,2},{2,3},{3,0},{4,5},{5,6},{6,7},{7,4},{8,9},{9,10},{10,1... | collective-permute-start | bytes 393224 | tf_op jit(solution)/shard_map/ppermute | solution.py:26
  148.8 8.9 %all-to-all-start.3 = ((f32[2,4,512]{2,0,1:T(2,128)}), f32[2,4,512]{2,0,1:T(2,128)S(1)}, u32[]{:S(2)}, u32[]{:S(2)}) async-start(f32[2,4,512]{2,0,1:T(2,128)} %pad_maximum_fusion.6), calls=%async_computation.3 | async-start | bytes 32768 | tf_op jit(solution)/shard_map/all_to_all | solution.py:138
  157.7 31.6 %all-to-all-start.2 = ((bf16[256,4,512]{2,0,1:T(8,128)(2,1)}), bf16[256,4,512]{2,0,1:T(8,128)(2,1)S(1)}, u32[]{:S(2)}, u32[]{:S(2)}) async-start(bf16[256,4,512]{2,0,1:T(8,128)(2,1)} %bitcast.167), calls=%async_computation.2 | async-start | bytes 2097152 | tf_op jit(solution)/shard_map/all_to_all | solution.py:130
Sparse Core Ops, SparseCore 0:
  9.6 44.3 all-gather.2
  59.6 36.5 all-reduce.6
